TPU v7x, 32 devices: a whole 2x2x4 slice. The times are simulated.
32 devices in a mesh: gy: 8 (over z, core), gx: 4 (over y, x).
Axes of the slice: x: 2, y: 2, z: 4, core: 2. Of those that a mesh axis runs over, the one named last changes fastest.
Arguments:
- ice_mask: int32 [512, 1024], P('gy', 'gx'), may hold values 0 or 1
- grounded: int32 [512, 1024], P('gy', 'gx'), may hold values 0 or 1
- thickness: float32 [512, 1024], P('gy', 'gx'), may hold values from 0.25 to 6
- friction: float32 [512, 1024], P('gy', 'gx'), may hold values from 0.3 to 3
- previous_velocity: float32 [2, 512, 1024], P(None, 'gy', 'gx'), may hold values from -6 to 6
- observed: float32 [2, 512, 1024], P(None, 'gy', 'gx'), may hold values from -6 to 6
- driving: float32 [2, 512, 1024], P(None, 'gy', 'gx'), may hold values from -6 to 6
Outputs:
- velocity: float32 [2, 512, 1024], P(None, 'gy', 'gx')
- adjoint: float32 [2, 512, 1024], P(None, 'gy', 'gx')
- friction_gradient: float32 [512, 1024], P('gy', 'gx')
All inputs are finite; a program needn't handle non-finite values. No bound on the sum of `ice_mask` or of `grounded` on one device may be relied on, other than what follows from the above.
Results may differ from a plain program's by a relative error of at most 0.00025.
Values sent between devices are 32-bit elements; how exact they have to be, the bound alone decides.
No kernel may reach another device: no remote copies, remote signals or barrier semaphores. Data moves between devices by JAX's collectives and lax.ppermute only.
A program may use at most 64 MiB of HBM per device.

v0:
```python
import jax
import jax.numpy as jnp
from jax import lax
from jax.sharding import PartitionSpec as P

ITERS = 2


def padded_2(shard, sides, width):
    for axis, dim in sides:
        count, length = (lax.axis_size(axis), shard.shape[dim])
        up = [(i, (i + 1) % count) for i in range(count - 1)]
        down = [(j, i) for i, j in up]
        last = lax.slice_in_dim(shard, length - width, length, axis=dim)
        first = lax.slice_in_dim(shard, 0, width, axis=dim)
        before = lax.ppermute(last, axis, up)
        after = lax.ppermute(first, axis, down)
        shard = jnp.concatenate([before, shard, after], axis=dim)
    return shard


def corner_dx(padded):
    return 0.5 * (
        padded[..., :-1, 1:] - padded[..., :-1, :-1] + padded[..., 1:, 1:] - padded[..., 1:, :-1]
    )


def corner_dy(padded):
    return 0.5 * (
        padded[..., 1:, :-1] - padded[..., :-1, :-1] + padded[..., 1:, 1:] - padded[..., :-1, 1:]
    )


def back_dx(stress):
    return 0.5 * (-stress[1:, 1:] + stress[1:, :-1] - stress[:-1, 1:] + stress[:-1, :-1])


def back_dy(stress):
    return 0.5 * (-stress[1:, 1:] - stress[1:, :-1] + stress[:-1, 1:] + stress[:-1, :-1])


def corner_weight(padded_vel, padded_thick):
    ux = corner_dx(padded_vel[0])
    uy = corner_dy(padded_vel[0])
    vx = corner_dx(padded_vel[1])
    vy = corner_dy(padded_vel[1])
    strain = ux * ux + vy * vy + ux * vy + 0.25 * (uy + vx) ** 2
    viscous = 0.5 * (strain + 0.01) ** (-1.0 / 3.0)
    mean_thick = 0.25 * (
        padded_thick[:-1, :-1]
        + padded_thick[:-1, 1:]
        + padded_thick[1:, :-1]
        + padded_thick[1:, 1:]
    )
    return mean_thick * viscous


def stress_div(padded, weight):
    ux = corner_dx(padded[0])
    uy = corner_dy(padded[0])
    vx = corner_dx(padded[1])
    vy = corner_dy(padded[1])
    s_ux = weight * (4.0 * ux + 2.0 * vy)
    s_vy = weight * (4.0 * vy + 2.0 * ux)
    s_shear = weight * (uy + vx)
    div_u = back_dx(s_ux) + back_dy(s_shear)
    div_v = back_dx(s_shear) + back_dy(s_vy)
    return jnp.stack([div_u, div_v], 0)


def shards(ice_mask, grounded, thickness, friction, previous_velocity, observed, driving):
    mask = ice_mask.astype(jnp.float32)
    fric = grounded.astype(jnp.float32) * friction
    start = mask * previous_velocity
    hm = mask * thickness
    res_a = mask * (start - observed)

    def finish(padded, field, weight):
        inner = padded[:, 1:-1, 1:-1]
        return mask * (stress_div(padded, weight) + fric * inner) + (1.0 - mask) * field

    def operate(field, weight):
        padded = padded_2(mask * field, (("gy", 1), ("gx", 2)), 1)
        return finish(padded, field, weight)

    def images(first, second, weight):
        return (operate(first, weight), operate(second, weight))

    def inner_sums(res_f, img_f, res_a, img_a):
        fwd_local = (jnp.sum(res_f * res_f), jnp.sum(res_f * img_f))
        adj_local = (jnp.sum(res_a * res_a), jnp.sum(res_a * img_a))
        fwd_total = lax.psum((fwd_local[0], fwd_local[1]), ("gy", "gx"))
        adj_total = lax.psum((adj_local[0], adj_local[1]), ("gy", "gx"))
        return ((fwd_total[0], fwd_total[1]), (adj_total[0], adj_total[1]))

    rims = padded_2(jnp.concatenate([start, hm[None]], 0), (("gy", 1), ("gx", 2)), 1)
    weight = corner_weight(rims[:2], rims[2])
    res_f = mask * driving - finish(rims[:2], start, weight)
    img_f, img_a = images(res_f, res_a, weight)
    velocity = start
    adjoint = jnp.zeros_like(start)
    (norm_f, prod_f), (norm_a, prod_a) = inner_sums(res_f, img_f, res_a, img_a)
    alpha_f = norm_f / prod_f
    alpha_a = norm_a / prod_a
    dir_f, along_f = (res_f, img_f)
    dir_a, along_a = (res_a, img_a)
    for step in range(ITERS):
        velocity = velocity + alpha_f * dir_f
        res_f = res_f - alpha_f * along_f
        adjoint = adjoint + alpha_a * dir_a
        res_a = res_a - alpha_a * along_a
        if step + 1 < ITERS:
            img_f, img_a = images(res_f, res_a, weight)
            (next_f, prod_f), (next_a, prod_a) = inner_sums(res_f, img_f, res_a, img_a)
            ratio_f = next_f / norm_f
            ratio_a = next_a / norm_a
            alpha_f = next_f / (prod_f - ratio_f * next_f / alpha_f)
            alpha_a = next_a / (prod_a - ratio_a * next_a / alpha_a)
            dir_f = res_f + ratio_f * dir_f
            along_f = img_f + ratio_f * along_f
            dir_a = res_a + ratio_a * dir_a
            along_a = img_a + ratio_a * along_a
            norm_f = next_f
            norm_a = next_a
    gradient = -mask * fric * (velocity[0] * adjoint[0] + velocity[1] * adjoint[1])
    return (velocity, adjoint, gradient)


def solution(mesh):
    placed = (
        P("gy", "gx"),
        P("gy", "gx"),
        P("gy", "gx"),
        P("gy", "gx"),
        P(None, "gy", "gx"),
        P(None, "gy", "gx"),
        P(None, "gy", "gx"),
    )
    return jax.shard_map(
        shards,
        mesh=mesh,
        in_specs=placed,
        out_specs=(P(None, "gy", "gx"), P(None, "gy", "gx"), P("gy", "gx")),
        check_vma=False,
    )
```

profile of v0, /device:TPU:0, one launch (start us, length us, event | category | flops | bytes accessed | tf_op | source)
XLA Modules:
  0.0 220.4 jit_solution(12335133444617943717)
XLA Ops:
  0.6 0.9 convert_element_type.6
  1.6 1.0 broadcast_multiply_fusion.1
  2.6 2.4 %collective-permute-start.12 = (f32[2,1,256]{2,1,0:T(1,128)S(1)}, f32[2,1,256]{2,1,0:T(1,128)S(1)}, u32[]{:S(2)}, u32[]{:S(2)}) collective-permute-start(f32[2,1,256]{2,1,0:T(1,128)S(1)} %get-tuple-element.80), channel_id=1, source_target_pairs={{0,4},{4,8},{8,12},{12,16},{16,20},{20,24},{24,28},{1,5},{5,9},{9,... | collective-permute-start | bytes 6152 | tf_op jit(solution)/shard_map/ppermute | solution.py:16
  4.9 1.3 collective-permute-start.13
  6.3 5.2 %collective-permute-start = (f32[3,1,256]{2,1,0:T(1,128)S(1)}, f32[3,1,256]{2,1,0:T(1,128)S(1)}, u32[]{:S(2)}, u32[]{:S(2)}) collective-permute-start(f32[3,1,256]{2,1,0:T(1,128)S(1)} %get-tuple-element.64), channel_id=1, source_target_pairs={{0,4},{4,8},{8,12},{12,16},{16,20},{20,24},{24,28},{1,5},{5,9},{9,... | collective-permute-start | bytes 9224 | tf_op jit(solution)/shard_map/ppermute | solution.py:16
  11.5 1.3 collective-permute-start.1
  13.0 3.4 %collective-permute-start.14 = (f32[2,66,1]{2,1,0:T(8,128)S(1)}, f32[2,66,1]{2,1,0:T(8,128)S(1)}, u32[]{:S(2)}, u32[]{:S(2)}) collective-permute-start(f32[2,66,1]{2,1,0:T(8,128)S(1)} %get-tuple-element.72), channel_id=1, source_target_pairs={{0,1},{1,2},{2,3},{4,5},{5,6},{6,7},{8,9},{9,10},{10,11},{12,13},{... | collective-permute-start | bytes 1592 | tf_op jit(solution)/shard_map/ppermute | solution.py:16
  16.4 1.3 collective-permute-start.15
  17.7 0.6 collective-permute-done.14
  18.3 4.3 %collective-permute-done.15 = f32[2,66,1]{2,1,0:T(8,128)S(1)} collective-permute-done((f32[2,66,1]{2,1,0:T(8,128)S(1)}, f32[2,66,1]{2,1,0:T(8,128)S(1)}, u32[]{:S(2)}, u32[]{:S(2)}) %collective-permute-start.15) | collective-permute-done | bytes 560 | tf_op jit(solution)/shard_map/ppermute | solution.py:17
  22.9 4.3 %collective-permute-start.2 = (f32[3,66,1]{2,1,0:T(8,128)S(1)}, f32[3,66,1]{2,1,0:T(8,128)S(1)}, u32[]{:S(2)}, u32[]{:S(2)}) collective-permute-start(f32[3,66,1]{2,1,0:T(8,128)S(1)} %get-tuple-element.58), channel_id=1, source_target_pairs={{0,1},{1,2},{2,3},{4,5},{5,6},{6,7},{8,9},{9,10},{10,11},{12,13},{... | collective-permute-start | bytes 2384 | tf_op jit(solution)/shard_map/ppermute | solution.py:16
  27.2 1.3 collective-permute-start.3
  28.6 2.1 collective-permute-done.2
  30.7 4.1 %collective-permute-done.3 = f32[3,66,1]{2,1,0:T(8,128)S(1)} collective-permute-done((f32[3,66,1]{2,1,0:T(8,128)S(1)}, f32[3,66,1]{2,1,0:T(8,128)S(1)}, u32[]{:S(2)}, u32[]{:S(2)}) %collective-permute-start.3) | collective-permute-done | bytes 824 | tf_op jit(solution)/shard_map/ppermute | solution.py:17
  34.8 0.2 pad_maximum_fusion
  35.0 0.5 add_multiply_fusion.3
  35.5 0.2 multiply_multiply_fusion.1
  35.7 0.2 fusion.31
  35.9 0.7 multiply_reduce_fusion.1
  36.5 41.3 %all-reduce.2 = (f32[]{:T(128)}, f32[]{:T(128)}) all-reduce(f32[]{:T(128)} %get-tuple-element.8, f32[]{:T(128)} %get-tuple-element.7), channel_id=1, replica_groups=mesh['gy'=8,'gx'=4] {'gy','gx'}, use_global_device_ids=true, to_apply=%region_9.0 | all-reduce | flops 2 | bytes 16 | tf_op jit(solution)/shard_map/psum | solution.py:93
  79.4 0.7 copy-done.3
  80.2 1.3 collective-permute-start.16
  81.5 1.3 collective-permute-start.17
  82.8 4.8 %collective-permute-start.4 = (f32[2,1,256]{2,1,0:T(1,128)S(1)}, f32[2,1,256]{2,1,0:T(1,128)S(1)}, u32[]{:S(2)}, u32[]{:S(2)}) collective-permute-start(f32[2,1,256]{2,1,0:T(1,128)S(1)} %get-tuple-element.78), channel_id=1, source_target_pairs={{0,4},{4,8},{8,12},{12,16},{16,20},{20,24},{24,28},{1,5},{5,9},{9,... | collective-permute-start | bytes 6152 | tf_op jit(solution)/shard_map/ppermute | solution.py:16
  87.6 1.3 collective-permute-start.5
  89.0 4.2 %collective-permute-start.18 = (f32[2,66,1]{2,1,0:T(8,128)S(1)}, f32[2,66,1]{2,1,0:T(8,128)S(1)}, u32[]{:S(2)}, u32[]{:S(2)}) collective-permute-start(f32[2,66,1]{2,1,0:T(8,128)S(1)} %get-tuple-element.68), channel_id=1, source_target_pairs={{0,1},{1,2},{2,3},{4,5},{5,6},{6,7},{8,9},{9,10},{10,11},{12,13},{... | collective-permute-start | bytes 1592 | tf_op jit(solution)/shard_map/ppermute | solution.py:16
  93.2 1.3 collective-permute-start.19
  94.6 4.5 %collective-permute-start.6 = (f32[2,66,1]{2,1,0:T(8,128)S(1)}, f32[2,66,1]{2,1,0:T(8,128)S(1)}, u32[]{:S(2)}, u32[]{:S(2)}) collective-permute-start(f32[2,66,1]{2,1,0:T(8,128)S(1)} %get-tuple-element.70), channel_id=1, source_target_pairs={{0,1},{1,2},{2,3},{4,5},{5,6},{6,7},{8,9},{9,10},{10,11},{12,13},{... | collective-permute-start | bytes 1592 | tf_op jit(solution)/shard_map/ppermute | solution.py:16
  99.2 1.3 collective-permute-start.7
  100.7 0.5 collective-permute-done.6
  101.2 4.8 %collective-permute-done.7 = f32[2,66,1]{2,1,0:T(8,128)S(1)} collective-permute-done((f32[2,66,1]{2,1,0:T(8,128)S(1)}, f32[2,66,1]{2,1,0:T(8,128)S(1)}, u32[]{:S(2)}, u32[]{:S(2)}) %collective-permute-start.7) | collective-permute-done | bytes 560 | tf_op jit(solution)/shard_map/ppermute | solution.py:17
  106.2 0.2 add_multiply_fusion.1
  106.4 0.2 add_multiply_fusion.7
  106.6 0.2 fusion.25
  106.8 0.2 fusion.43
  107.0 0.8 fusion.14
  107.8 42.9 %all-reduce.1 = (f32[]{:T(128)}, f32[]{:T(128)}) all-reduce(f32[]{:T(128)} %get-tuple-element.5, f32[]{:T(128)} %get-tuple-element.4), channel_id=1, replica_groups=mesh['gy'=8,'gx'=4] {'gy','gx'}, use_global_device_ids=true, to_apply=%region_1.0 | all-reduce | flops 2 | bytes 16 | tf_op jit(solution)/shard_map/psum | solution.py:92
  152.0 1.3 collective-permute-start.8
  153.3 1.3 collective-permute-start.9
  154.6 2.5 %collective-permute-done.9 = f32[2,1,256]{2,1,0:T(1,128)S(1)} collective-permute-done((f32[2,1,256]{2,1,0:T(1,128)S(1)}, f32[2,1,256]{2,1,0:T(1,128)S(1)}, u32[]{:S(2)}, u32[]{:S(2)}) %collective-permute-start.9) | collective-permute-done | bytes 2080 | tf_op jit(solution)/shard_map/ppermute | solution.py:17
  157.2 4.2 %collective-permute-start.10 = (f32[2,66,1]{2,1,0:T(8,128)S(1)}, f32[2,66,1]{2,1,0:T(8,128)S(1)}, u32[]{:S(2)}, u32[]{:S(2)}) collective-permute-start(f32[2,66,1]{2,1,0:T(8,128)S(1)} %get-tuple-element.66), channel_id=1, source_target_pairs={{0,1},{1,2},{2,3},{4,5},{5,6},{6,7},{8,9},{9,10},{10,11},{12,13},{... | collective-permute-start | bytes 1592 | tf_op jit(solution)/shard_map/ppermute | solution.py:16
  161.3 1.3 collective-permute-start.11
  162.6 0.7 collective-permute-done.10
  163.3 4.3 %collective-permute-done.11 = f32[2,66,1]{2,1,0:T(8,128)S(1)} collective-permute-done((f32[2,66,1]{2,1,0:T(8,128)S(1)}, f32[2,66,1]{2,1,0:T(8,128)S(1)}, u32[]{:S(2)}, u32[]{:S(2)}) %collective-permute-start.11) | collective-permute-done | bytes 560 | tf_op jit(solution)/shard_map/ppermute | solution.py:17
  167.8 0.2 add_multiply_fusion.5
  168.2 0.7 fusion.8
  168.9 41.8 %all-reduce = (f32[]{:T(128)}, f32[]{:T(128)}, f32[]{:T(128)}, f32[]{:T(128)}) all-reduce(f32[]{:T(128)} %get-tuple-element.10, f32[]{:T(128)} %get-tuple-element.9, f32[]{:T(128)} %get-tuple-element.6, f32[]{:T(128)} %get-tuple-element.3), channel_id=1, replica_groups=mesh['gy'=8,'gx'=4] {'gy','gx'}, use_global_device_ids=true, to_apply=%region_5.0 | all-reduce | flops 4 | bytes 32 | tf_op jit(solution)/shard_map/psum | solution.py:92
  219.7 0.7 fusion.19
  (59 shorter events, 2.0 us)
Async XLA Ops:
  0.6 0.9 copy-start.4
  1.6 4.7 %copy-start = (s32[64,256]{1,0:T(8,128)S(1)}, s32[64,256]{1,0:T(8,128)}, u32[]{:S(2)}) copy-start(s32[64,256]{1,0:T(8,128)} %param.7) | copy-start | bytes 196612
  1.6 4.7 %copy-start.7 = (f32[64,256]{1,0:T(8,128)S(1)}, f32[64,256]{1,0:T(8,128)}, u32[]{:S(2)}) copy-start(f32[64,256]{1,0:T(8,128)} %param.9) | copy-start | bytes 196612
  2.6 10.3 %collective-permute-start.12 = (f32[2,1,256]{2,1,0:T(1,128)S(1)}, f32[2,1,256]{2,1,0:T(1,128)S(1)}, u32[]{:S(2)}, u32[]{:S(2)}) collective-permute-start(f32[2,1,256]{2,1,0:T(1,128)S(1)} %get-tuple-element.80), channel_id=1, source_target_pairs={{0,4},{4,8},{8,12},{12,16},{16,20},{20,24},{24,28},{1,5},{5,9},{9,... | collective-permute-start | bytes 6152 | tf_op jit(solution)/shard_map/ppermute | solution.py:16
  4.9 7.9 %collective-permute-start.13 = (f32[2,1,256]{2,1,0:T(1,128)S(1)}, f32[2,1,256]{2,1,0:T(1,128)S(1)}, u32[]{:S(2)}, u32[]{:S(2)}) collective-permute-start(f32[2,1,256]{2,1,0:T(1,128)S(1)} %get-tuple-element.81), channel_id=1, source_target_pairs={{4,0},{8,4},{12,8},{16,12},{20,16},{24,20},{28,24},{5,1},{9,5},{13... | collective-permute-start | bytes 6152 | tf_op jit(solution)/shard_map/ppermute | solution.py:17
  6.3 16.5 %collective-permute-start = (f32[3,1,256]{2,1,0:T(1,128)S(1)}, f32[3,1,256]{2,1,0:T(1,128)S(1)}, u32[]{:S(2)}, u32[]{:S(2)}) collective-permute-start(f32[3,1,256]{2,1,0:T(1,128)S(1)} %get-tuple-element.64), channel_id=1, source_target_pairs={{0,4},{4,8},{8,12},{12,16},{16,20},{20,24},{24,28},{1,5},{5,9},{9,... | collective-permute-start | bytes 9224 | tf_op jit(solution)/shard_map/ppermute | solution.py:16
  11.5 11.3 %collective-permute-start.1 = (f32[3,1,256]{2,1,0:T(1,128)S(1)}, f32[3,1,256]{2,1,0:T(1,128)S(1)}, u32[]{:S(2)}, u32[]{:S(2)}) collective-permute-start(f32[3,1,256]{2,1,0:T(1,128)S(1)} %get-tuple-element.65), channel_id=1, source_target_pairs={{4,0},{8,4},{12,8},{16,12},{20,16},{24,20},{28,24},{5,1},{9,5},{13... | collective-permute-start | bytes 9224 | tf_op jit(solution)/shard_map/ppermute | solution.py:17
  12.9 4.8 %copy-start.5 = (f32[64,256]{1,0:T(8,128)S(1)}, f32[64,256]{1,0:T(8,128)}, u32[]{:S(2)}) copy-start(f32[64,256]{1,0:T(8,128)} %param.10) | copy-start | bytes 196612
  12.9 4.8 %copy-start.6 = (s32[64,256]{1,0:T(8,128)S(1)}, s32[64,256]{1,0:T(8,128)}, u32[]{:S(2)}) copy-start(s32[64,256]{1,0:T(8,128)} %param.8) | copy-start | bytes 196612
  13.0 5.4 %collective-permute-start.14 = (f32[2,66,1]{2,1,0:T(8,128)S(1)}, f32[2,66,1]{2,1,0:T(8,128)S(1)}, u32[]{:S(2)}, u32[]{:S(2)}) collective-permute-start(f32[2,66,1]{2,1,0:T(8,128)S(1)} %get-tuple-element.72), channel_id=1, source_target_pairs={{0,1},{1,2},{2,3},{4,5},{5,6},{6,7},{8,9},{9,10},{10,11},{12,13},{... | collective-permute-start | bytes 1592 | tf_op jit(solution)/shard_map/ppermute | solution.py:16
  16.4 6.2 %collective-permute-start.15 = (f32[2,66,1]{2,1,0:T(8,128)S(1)}, f32[2,66,1]{2,1,0:T(8,128)S(1)}, u32[]{:S(2)}, u32[]{:S(2)}) collective-permute-start(f32[2,66,1]{2,1,0:T(8,128)S(1)} %get-tuple-element.73), channel_id=1, source_target_pairs={{1,0},{2,1},{3,2},{5,4},{6,5},{7,6},{9,8},{10,9},{11,10},{13,12},{... | collective-permute-start | bytes 1592 | tf_op jit(solution)/shard_map/ppermute | solution.py:17
  22.9 7.7 %collective-permute-start.2 = (f32[3,66,1]{2,1,0:T(8,128)S(1)}, f32[3,66,1]{2,1,0:T(8,128)S(1)}, u32[]{:S(2)}, u32[]{:S(2)}) collective-permute-start(f32[3,66,1]{2,1,0:T(8,128)S(1)} %get-tuple-element.58), channel_id=1, source_target_pairs={{0,1},{1,2},{2,3},{4,5},{5,6},{6,7},{8,9},{9,10},{10,11},{12,13},{... | collective-permute-start | bytes 2384 | tf_op jit(solution)/shard_map/ppermute | solution.py:16
  27.2 7.5 %collective-permute-start.3 = (f32[3,66,1]{2,1,0:T(8,128)S(1)}, f32[3,66,1]{2,1,0:T(8,128)S(1)}, u32[]{:S(2)}, u32[]{:S(2)}) collective-permute-start(f32[3,66,1]{2,1,0:T(8,128)S(1)} %get-tuple-element.59), channel_id=1, source_target_pairs={{1,0},{2,1},{3,2},{5,4},{6,5},{7,6},{9,8},{10,9},{11,10},{13,12},{... | collective-permute-start | bytes 2384 | tf_op jit(solution)/shard_map/ppermute | solution.py:17
  79.2 0.9 copy-start.3
  80.2 8.7 %collective-permute-start.16 = (f32[2,1,256]{2,1,0:T(1,128)S(1)}, f32[2,1,256]{2,1,0:T(1,128)S(1)}, u32[]{:S(2)}, u32[]{:S(2)}) collective-permute-start(f32[2,1,256]{2,1,0:T(1,128)S(1)} %get-tuple-element.76), channel_id=1, source_target_pairs={{0,4},{4,8},{8,12},{12,16},{16,20},{20,24},{24,28},{1,5},{5,9},{9,... | collective-permute-start | bytes 6152 | tf_op jit(solution)/shard_map/ppermute | solution.py:16
  81.5 7.4 %collective-permute-start.17 = (f32[2,1,256]{2,1,0:T(1,128)S(1)}, f32[2,1,256]{2,1,0:T(1,128)S(1)}, u32[]{:S(2)}, u32[]{:S(2)}) collective-permute-start(f32[2,1,256]{2,1,0:T(1,128)S(1)} %get-tuple-element.77), channel_id=1, source_target_pairs={{4,0},{8,4},{12,8},{16,12},{20,16},{24,20},{28,24},{5,1},{9,5},{13... | collective-permute-start | bytes 6152 | tf_op jit(solution)/shard_map/ppermute | solution.py:17
  82.8 11.7 %collective-permute-start.4 = (f32[2,1,256]{2,1,0:T(1,128)S(1)}, f32[2,1,256]{2,1,0:T(1,128)S(1)}, u32[]{:S(2)}, u32[]{:S(2)}) collective-permute-start(f32[2,1,256]{2,1,0:T(1,128)S(1)} %get-tuple-element.78), channel_id=1, source_target_pairs={{0,4},{4,8},{8,12},{12,16},{16,20},{20,24},{24,28},{1,5},{5,9},{9,... | collective-permute-start | bytes 6152 | tf_op jit(solution)/shard_map/ppermute | solution.py:16
  87.6 6.9 %collective-permute-start.5 = (f32[2,1,256]{2,1,0:T(1,128)S(1)}, f32[2,1,256]{2,1,0:T(1,128)S(1)}, u32[]{:S(2)}, u32[]{:S(2)}) collective-permute-start(f32[2,1,256]{2,1,0:T(1,128)S(1)} %get-tuple-element.79), channel_id=1, source_target_pairs={{4,0},{8,4},{12,8},{16,12},{20,16},{24,20},{28,24},{5,1},{9,5},{13... | collective-permute-start | bytes 6152 | tf_op jit(solution)/shard_map/ppermute | solution.py:17
  89.0 11.5 %collective-permute-start.18 = (f32[2,66,1]{2,1,0:T(8,128)S(1)}, f32[2,66,1]{2,1,0:T(8,128)S(1)}, u32[]{:S(2)}, u32[]{:S(2)}) collective-permute-start(f32[2,66,1]{2,1,0:T(8,128)S(1)} %get-tuple-element.68), channel_id=1, source_target_pairs={{0,1},{1,2},{2,3},{4,5},{5,6},{6,7},{8,9},{9,10},{10,11},{12,13},{... | collective-permute-start | bytes 1592 | tf_op jit(solution)/shard_map/ppermute | solution.py:16
  93.2 7.3 %collective-permute-start.19 = (f32[2,66,1]{2,1,0:T(8,128)S(1)}, f32[2,66,1]{2,1,0:T(8,128)S(1)}, u32[]{:S(2)}, u32[]{:S(2)}) collective-permute-start(f32[2,66,1]{2,1,0:T(8,128)S(1)} %get-tuple-element.69), channel_id=1, source_target_pairs={{1,0},{2,1},{3,2},{5,4},{6,5},{7,6},{9,8},{10,9},{11,10},{13,12},{... | collective-permute-start | bytes 1592 | tf_op jit(solution)/shard_map/ppermute | solution.py:17
  94.6 6.5 %collective-permute-start.6 = (f32[2,66,1]{2,1,0:T(8,128)S(1)}, f32[2,66,1]{2,1,0:T(8,128)S(1)}, u32[]{:S(2)}, u32[]{:S(2)}) collective-permute-start(f32[2,66,1]{2,1,0:T(8,128)S(1)} %get-tuple-element.70), channel_id=1, source_target_pairs={{0,1},{1,2},{2,3},{4,5},{5,6},{6,7},{8,9},{9,10},{10,11},{12,13},{... | collective-permute-start | bytes 1592 | tf_op jit(solution)/shard_map/ppermute | solution.py:16
  99.2 6.8 %collective-permute-start.7 = (f32[2,66,1]{2,1,0:T(8,128)S(1)}, f32[2,66,1]{2,1,0:T(8,128)S(1)}, u32[]{:S(2)}, u32[]{:S(2)}) collective-permute-start(f32[2,66,1]{2,1,0:T(8,128)S(1)} %get-tuple-element.71), channel_id=1, source_target_pairs={{1,0},{2,1},{3,2},{5,4},{6,5},{7,6},{9,8},{10,9},{11,10},{13,12},{... | collective-permute-start | bytes 1592 | tf_op jit(solution)/shard_map/ppermute | solution.py:17
  152.0 2.6 %collective-permute-start.8 = (f32[2,1,256]{2,1,0:T(1,128)S(1)}, f32[2,1,256]{2,1,0:T(1,128)S(1)}, u32[]{:S(2)}, u32[]{:S(2)}) collective-permute-start(f32[2,1,256]{2,1,0:T(1,128)S(1)} %get-tuple-element.74), channel_id=1, source_target_pairs={{0,4},{4,8},{8,12},{12,16},{16,20},{20,24},{24,28},{1,5},{5,9},{9,... | collective-permute-start | bytes 6152 | tf_op jit(solution)/shard_map/ppermute | solution.py:16
  153.3 3.8 %collective-permute-start.9 = (f32[2,1,256]{2,1,0:T(1,128)S(1)}, f32[2,1,256]{2,1,0:T(1,128)S(1)}, u32[]{:S(2)}, u32[]{:S(2)}) collective-permute-start(f32[2,1,256]{2,1,0:T(1,128)S(1)} %get-tuple-element.75), channel_id=1, source_target_pairs={{4,0},{8,4},{12,8},{16,12},{20,16},{24,20},{28,24},{5,1},{9,5},{13... | collective-permute-start | bytes 6152 | tf_op jit(solution)/shard_map/ppermute | solution.py:17
  157.2 6.1 %collective-permute-start.10 = (f32[2,66,1]{2,1,0:T(8,128)S(1)}, f32[2,66,1]{2,1,0:T(8,128)S(1)}, u32[]{:S(2)}, u32[]{:S(2)}) collective-permute-start(f32[2,66,1]{2,1,0:T(8,128)S(1)} %get-tuple-element.66), channel_id=1, source_target_pairs={{0,1},{1,2},{2,3},{4,5},{5,6},{6,7},{8,9},{9,10},{10,11},{12,13},{... | collective-permute-start | bytes 1592 | tf_op jit(solution)/shard_map/ppermute | solution.py:16
  161.3 6.2 %collective-permute-start.11 = (f32[2,66,1]{2,1,0:T(8,128)S(1)}, f32[2,66,1]{2,1,0:T(8,128)S(1)}, u32[]{:S(2)}, u32[]{:S(2)}) collective-permute-start(f32[2,66,1]{2,1,0:T(8,128)S(1)} %get-tuple-element.67), channel_id=1, source_target_pairs={{1,0},{2,1},{3,2},{5,4},{6,5},{7,6},{9,8},{10,9},{11,10},{13,12},{... | collective-permute-start | bytes 1592 | tf_op jit(solution)/shard_map/ppermute | solution.py:17
  219.7 0.7 copy-start.1
  219.7 0.7 copy-start.2
where the time goes:
time: 222 us; the launch traced here: 220 us
  blocking collectives  126 us (57%)
  starting transfers between devices  48.5 us (22%)
  waiting for transfers between devices  23.8 us (11%)
  between operations  12.7 us (6%)
  other arithmetic  8.04 us (4%)
    psum x2, blocking collectives, inner_sums(): fwd_total = lax.psum((fwd_local[0], fwd_local[1]), ('gy', 'gx'))  84.7 us
    psum x1, blocking collectives, inner_sums(): adj_total = lax.psum((adj_local[0], adj_local[1]), ('gy', 'gx'))  41.3 us
    ppermute x10, starting transfers between devices, padded_2(): before = lax.ppermute(last, axis, up)  35.5 us
    ppermute x10, waiting for transfers between devices, padded_2(): after = lax.ppermute(first, axis, down)  20 us
    ppermute x10, starting transfers between devices, padded_2(): after = lax.ppermute(first, axis, down)  12.9 us
  transfers between devices with their start and end apart: 20, of which 9 were waited for; matrix products, arithmetic and copies ran while one was open for 0% of the time, Pallas kernels for 0%

commit v1 on v0

v1 whole, which is shorter than its diff:
```python
import functools

import jax
import jax.numpy as jnp
from jax import lax
from jax.experimental import pallas as pl
from jax.experimental.pallas import tpu as pltpu
from jax.sharding import PartitionSpec as P

LANES = 128
TILE = 8
BELOW = 3
ABOVE = 2
SLOT = BELOW
FIELDS = 8
GROUPS = LANES // (SLOT * FIELDS)
VMEM_LIMIT = 32 * 1024 * 1024


def derive(ice, grounded, thick, fric, prev, obs, drv):
    mask = ice.astype(jnp.float32)
    start_u = mask * prev[0]
    start_v = mask * prev[1]
    coef = mask * (grounded.astype(jnp.float32) * fric) + (1.0 - mask)
    return (
        start_u,
        start_v,
        mask * thick,
        coef,
        mask * drv[0],
        mask * drv[1],
        mask * (start_u - obs[0]),
        mask * (start_v - obs[1]),
    )


def read(refs, at):
    return [r[at, :] if len(r.shape) == 2 else r[:, at, :] for r in refs]


def pack_rows_kernel(*refs):
    raw, (down, up), held, arrived = refs[:7], refs[7:9], refs[9:16], refs[16]
    copies = [pltpu.make_async_copy(src, dst, arrived.at[i]) for i, (src, dst) in enumerate(zip(raw, held))]
    for copy in copies:
        copy.start()
    for copy in copies:
        copy.wait()
    rows = held[0].shape[0]
    for f, field in enumerate(derive(*read(held, pl.ds(0, TILE)))):
        up[BELOW * f : BELOW * (f + 1), :] = field[:BELOW]
    for f, field in enumerate(derive(*read(held, pl.ds(rows - TILE, TILE)))):
        down[ABOVE * f : ABOVE * (f + 1), :] = field[TILE - ABOVE :]


def add_columns(blocks, tile, fields):
    group, at_row, lane = *divmod(tile, blocks["tiles"]), blocks["lane"]
    for f, (first, last) in enumerate(fields):
        at = SLOT * (FIELDS * group + f)
        mine = (lane >= at) & (lane < at + ABOVE)
        east = pltpu.roll(last, (at + ABOVE) % LANES, 1)
        blocks["east"][at_row] = jnp.where(mine, east, blocks["east"][at_row])
        mine = (lane >= at) & (lane < at + BELOW)
        west = pltpu.roll(first, at % LANES, 1)
        blocks["west"][at_row] = jnp.where(mine, west, blocks["west"][at_row])


def new_blocks(east, west):
    lane = lax.broadcasted_iota(jnp.int32, (TILE, LANES), 1)
    return {"tiles": len(east), "lane": lane, "east": east, "west": west}


def block_tiles(rows):
    return -(-(rows // TILE + 1) // GROUPS)


def fields_kernel(*refs):
    raw = refs[:7]
    own, east, west = refs[7:]
    rows, cols = own.shape[1:]
    count = block_tiles(rows)
    none = jnp.zeros((TILE, LANES), jnp.float32)
    blocks = new_blocks([none] * count, [none] * count)
    for tile in range(rows // TILE):
        at = pl.ds(TILE * tile, TILE)
        fields = derive(*read(raw, at))
        for f, field in enumerate(fields):
            own[f, at, :] = field
        add_columns(blocks, tile, [(x[:, :LANES], x[:, cols - LANES :]) for x in fields])
    for i in range(count):
        at = pl.ds(TILE * i, TILE)
        east[at, :], west[at, :] = blocks["east"][i], blocks["west"][i]


def tail_kernel(own_tiles, above, below, east_own, west_own, tail, sends):
    cols = tail.shape[2]
    height = east_own.shape[0]
    for f in range(FIELDS):
        tail[f, 0:BELOW, :] = below[BELOW * f : BELOW * (f + 1), :]
        tail[f, BELOW : TILE - ABOVE, :] = jnp.zeros((TILE - ABOVE - BELOW, cols), jnp.float32)
        tail[f, TILE - ABOVE : TILE, :] = above[ABOVE * f : ABOVE * (f + 1), :]
    at = [pl.ds(TILE * i, TILE) for i in range(height // TILE)]
    blocks = new_blocks([east_own[a, :] for a in at], [west_own[a, :] for a in at])
    add_columns(blocks, own_tiles, [(tail[f, :, :LANES], tail[f, :, cols - LANES :]) for f in range(FIELDS)])
    gx, count = lax.axis_index("gx"), lax.axis_size("gx")
    for i in range(count):
        to_next, to_previous = gx + 1 == i, gx - 1 == i
        for j in range(height // TILE):
            block = jnp.where(to_next, blocks["east"][j], jnp.where(to_previous, blocks["west"][j], 0.0))
            sends[pl.ds(height * i + TILE * j, TILE), :] = block


def to_right(x):
    return pltpu.roll(x, x.shape[1] - 1, 1)


def to_left(x):
    return pltpu.roll(x, 1, 1)


def gradient(u0, u1, v0, v1):
    us, ud = u1 + u0, u1 - u0
    vs, vd = v1 + v0, v1 - v0
    ux = to_right(us) - us
    uy = to_right(ud) + ud
    vx = to_right(vs) - vs
    vy = to_right(vd) + vd
    return ux, uy, vx, vy


def stress_of(weight, ux, vy, shear):
    return weight * (4.0 * ux + 2.0 * vy), weight * (4.0 * vy + 2.0 * ux), weight * shear


def solve_kernel(own, tail, columns, out, sums, fld, wgt, wown, strs, res, img, grd):
    rows, cols = own.shape[1:]
    wide = cols + LANES
    ring = rows + TILE
    tiles = ring // TILE
    gy, gx = lax.axis_index("gy"), lax.axis_index("gx")

    lane = lax.broadcasted_iota(jnp.int32, (TILE, LANES), 1)
    from_right, from_left = lane < BELOW, lane >= LANES - ABOVE
    count = block_tiles(rows)
    gx_last = lax.axis_size("gx") - 1
    before = jnp.maximum(gx - 1, 0) * (TILE * count)
    after = jnp.minimum(gx + 1, gx_last) * (TILE * count)
    left, right = [], []
    for i in range(count):
        block = columns[pl.ds(pl.multiple_of(before + TILE * i, TILE), TILE), :]
        left.append(jnp.where(gx > 0, block, 0.0))
        block = columns[pl.ds(pl.multiple_of(after + TILE * i, TILE), TILE), :]
        right.append(jnp.where(gx < gx_last, block, 0.0))
    for t in range(tiles):
        at = pl.ds(TILE * t, TILE)
        group, i = divmod(t, count)
        for f in range(FIELDS):
            lanes = SLOT * (FIELDS * group + f)
            body = own[f, at, :] if t < tiles - 1 else tail[f]
            side = jnp.where(from_left, pltpu.roll(left[i], (2 * LANES - ABOVE - lanes) % LANES, 1), 0.0)
            side = jnp.where(from_right, pltpu.roll(right[i], (LANES - lanes) % LANES, 1), side)
            fld[f, at, :cols] = body
            fld[f, at, cols:] = side
    for f in range(3):
        fld[f, ring : ring + 1, :] = fld[f, 0:1, :]

    def pair(ref, f, t):
        return ref[f, pl.ds(TILE * t, TILE), :], ref[f, pl.ds(TILE * t + 1, TILE), :]

    def put_stress(which, t, parts):
        for i, part in enumerate(parts):
            strs[3 * which + i, pl.ds(TILE * t + TILE, TILE), :] = part
            if t == tiles - 1:
                strs[3 * which + i, TILE - 1 : TILE, :] = part[TILE - 1 :, :]

    def divergence(which, t):
        ux0, vy0, sh0 = [strs[3 * which + i, pl.ds(TILE * t + TILE, TILE), :] for i in range(3)]
        ux1, vy1, sh1 = [strs[3 * which + i, pl.ds(TILE * t + TILE - 1, TILE), :] for i in range(3)]
        a, b = ux0 + ux1, sh1 - sh0
        div_u = (b - a) + to_left(a + b)
        a, b = sh0 + sh1, vy1 - vy0
        div_v = (b - a) + to_left(a + b)
        return div_u, div_v

    def operator(which, t, u, v):
        at = pl.ds(TILE * t, TILE)
        ice = fld[2, at, :] > 0.0
        coef = fld[3, at, :]
        div_u, div_v = divergence(which, t)
        return jnp.where(ice, div_u, 0.0) + coef * u, jnp.where(ice, div_v, 0.0) + coef * v

    row_of = lax.broadcasted_iota(jnp.int32, (TILE, wide), 0)
    col_of = lax.broadcasted_iota(jnp.int32, (TILE, wide), 1)
    own_col = (col_of < cols) | ((col_of == wide - 1) & (gx == 0))
    own_tail = own_col & (row_of == TILE - 1) & (gy == 0)

    for t in range(tiles):
        at = pl.ds(TILE * t, TILE)
        ux, uy, vx, vy = gradient(*pair(fld, 0, t), *pair(fld, 1, t))
        h0, h1 = pair(fld, 2, t)
        hs = h0 + h1
        hs = hs + to_right(hs)
        shear = uy + vx
        strain = ux * ux + vy * vy + ux * vy + 0.25 * (shear * shear)
        weight = (hs * 0.03125) * jnp.exp(jnp.log(0.25 * strain + 0.01) * (-1.0 / 3.0))
        wgt[at, :] = weight
        wown[at, :] = jnp.where(own_col if t < tiles - 1 else own_tail, weight, 0.0)
        put_stress(0, t, stress_of(weight, ux, vy, shear))

    for t in range(tiles):
        at = pl.ds(TILE * t, TILE)
        image = operator(0, t, fld[0, at, :], fld[1, at, :])
        for i in range(2):
            res[i, at, :] = fld[4 + i, at, :] - image[i]
            res[2 + i, at, :] = fld[6 + i, at, :]
    for i in range(4):
        res[i, ring : ring + 1, :] = res[i, 0:1, :]

    for t in range(tiles):
        at = pl.ds(TILE * t, TILE)
        weight = wgt[at, :]
        for s in range(2):
            ux, uy, vx, vy = gradient(*pair(res, 2 * s, t), *pair(res, 2 * s + 1, t))
            shear = uy + vx
            grd[3 * s, at, :], grd[3 * s + 1, at, :], grd[3 * s + 2, at, :] = ux, vy, shear
            put_stress(s, t, stress_of(weight, ux, vy, shear))
    dots = [jnp.zeros((TILE, cols), jnp.float32) for _ in range(4)]
    for t in range(tiles):
        at = pl.ds(TILE * t, TILE)
        for s in range(2):
            r = [res[2 * s + i, at, :] for i in range(2)]
            q = operator(s, t, *r)
            for i in range(2):
                img[2 * s + i, at, :] = q[i]
                if t < tiles - 1:
                    r_own, q_own = r[i][:, :cols], q[i][:, :cols]
                    out[4 * s + i, at, :] = r_own
                    out[4 * s + 2 + i, at, :] = q_own
                    dots[2 * s] = dots[2 * s] + r_own * r_own
                    dots[2 * s + 1] = dots[2 * s + 1] + r_own * q_own
    for i in range(4):
        img[i, ring : ring + 1, :] = img[i, 0:1, :]

    def total(x):
        return jnp.sum(jnp.sum(x, axis=0, keepdims=True), axis=1, keepdims=True)

    dots = [total(x) for x in dots]
    theta = []
    for s in range(2):
        some = dots[2 * s] > 0.0
        theta.append(jnp.where(some, dots[2 * s + 1] / jnp.where(some, dots[2 * s], 1.0), 0.0))

    size = [jnp.zeros((TILE, cols), jnp.float32) for _ in range(2)]
    cells = [[jnp.zeros((TILE, cols), jnp.float32) for _ in range(3)] for _ in range(2)]
    energy = [[jnp.zeros((TILE, wide), jnp.float32) for _ in range(3)] for _ in range(2)]
    for t in range(tiles):
        at = pl.ds(TILE * t, TILE)
        weight = wown[at, :]
        for s in range(2):
            ux, uy, vx, vy = gradient(*pair(img, 2 * s, t), *pair(img, 2 * s + 1, t))
            rx, ry, rs = [grd[3 * s + i, at, :] for i in range(3)]
            wx, wy, ws = ux - theta[s] * rx, vy - theta[s] * ry, (uy + vx) - theta[s] * rs
            sx, sy, ss = stress_of(weight, wx, wy, ws)
            energy[s][0] = energy[s][0] + (sx * wx + sy * wy + ss * ws)
            energy[s][1] = energy[s][1] + (sx * rx + sy * ry + ss * rs)
            sx, sy, ss = stress_of(weight, rx, ry, rs)
            energy[s][2] = energy[s][2] + (sx * rx + sy * ry + ss * rs)
            if t < tiles - 1:
                coef = fld[3, at, :cols]
                for i in range(2):
                    r = res[2 * s + i, at, :cols]
                    w = img[2 * s + i, at, :cols] - theta[s] * r
                    size[s] = size[s] + w * w
                    cells[s][0] = cells[s][0] + coef * (w * w)
                    cells[s][1] = cells[s][1] + coef * (w * r)
                    cells[s][2] = cells[s][2] + coef * (r * r)
    values = []
    for s in range(2):
        values += [dots[2 * s], dots[2 * s + 1], total(size[s])]
        values += [total(energy[s][i]) + total(cells[s][i]) for i in range(3)]
    lane = lax.broadcasted_iota(jnp.int32, (1, LANES), 1)
    row = jnp.zeros((1, LANES), jnp.float32)
    for i, value in enumerate(values):
        row = jnp.where(lane == i, value, row)
    sums[...] = jnp.broadcast_to(row, sums.shape)


def steps_of(table, first):
    norm_d, prod_d, size_d, ww, rw, rr = [table[:, first + i : first + i + 1] for i in range(6)]

    def over(x):
        return jnp.sum(x, axis=0, keepdims=True)

    norm, prod = over(norm_d), over(prod_d)
    alpha = norm / prod
    theta = prod / norm
    some = norm_d > 0.0
    shift = jnp.where(some, prod_d / jnp.where(some, norm_d, 1.0), 0.0) - theta
    square = alpha * alpha
    norm_1 = square * over(size_d + shift * shift * norm_d)
    prod_1 = square * over(ww + shift * (2.0 * rw + shift * rr))
    ratio = norm_1 / norm
    some = norm_1 > 0.0
    bottom = jnp.where(some, prod_1 - ratio * norm_1 / alpha, 1.0)
    return alpha, ratio, norm_1 / bottom


def finish_kernel(table, own, vectors, velocity, adjoint, grad):
    steps = [steps_of(table[...], 6 * s) for s in range(2)]
    rows = own.shape[1]
    for row in range(0, rows, TILE):
        at = pl.ds(row, TILE)
        made = []
        for s in range(2):
            alpha, ratio, alpha_1 = steps[s]
            for i in range(2):
                r, q = vectors[4 * s + i, at, :], vectors[4 * s + 2 + i, at, :]
                step = alpha * r + alpha_1 * ((r - alpha * q) + ratio * r)
                made.append(own[i, at, :] + step if s == 0 else step)
        friction = jnp.where(own[2, at, :] > 0.0, own[3, at, :], 0.0)
        velocity[0, at, :], velocity[1, at, :] = made[0], made[1]
        adjoint[0, at, :], adjoint[1, at, :] = made[2], made[3]
        grad[at, :] = -friction * (made[0] * made[2] + made[1] * made[3])


def shape(*dims):
    return jax.ShapeDtypeStruct(dims, jnp.float32)


def call(kernel, outs, scratch=(), **kwargs):
    return pl.pallas_call(
        kernel,
        out_shape=outs,
        scratch_shapes=scratch,
        compiler_params=pltpu.CompilerParams(vmem_limit_bytes=VMEM_LIMIT),
        **kwargs,
    )


def swap(to_next, to_previous, axis):
    count = lax.axis_size(axis)
    ahead = [(i, i + 1) for i in range(count - 1)]
    back = [(i + 1, i) for i in range(count - 1)]
    return lax.ppermute(to_next, axis, ahead), lax.ppermute(to_previous, axis, back)


def shards(ice_mask, grounded, thickness, friction, previous_velocity, observed, driving):
    raw = (ice_mask, grounded, thickness, friction, previous_velocity, observed, driving)
    rows, cols = ice_mask.shape
    wide, ring = cols + LANES, rows + TILE
    devices = lax.axis_size(("gy", "gx"))
    height = TILE * block_tiles(rows)
    down, up, *held = call(
        pack_rows_kernel,
        (shape(ABOVE * FIELDS, cols), shape(BELOW * FIELDS, cols), *[jax.ShapeDtypeStruct(x.shape, x.dtype) for x in raw]),
        scratch=(pltpu.SemaphoreType.DMA((len(raw),)),),
        in_specs=[pl.BlockSpec(memory_space=pltpu.HBM)] * len(raw),
        name="pack_rows",
    )(*[pltpu.with_memory_space_constraint(x, pltpu.HBM) for x in raw])
    above, below = swap(down, up, "gy")
    own, east_own, west_own = call(
        fields_kernel,
        (shape(FIELDS, rows, cols), shape(height, LANES), shape(height, LANES)),
        name="fields",
        cost_estimate=pl.CostEstimate(flops=40 * rows * cols, bytes_accessed=18 * 4 * rows * cols, transcendentals=0),
    )(*held)
    tail, sends = call(
        functools.partial(tail_kernel, rows // TILE),
        (shape(FIELDS, TILE, cols), shape(lax.axis_size("gx") * height, LANES)),
        name="tail",
    )(above, below, east_own, west_own)
    columns = lax.all_to_all(sends, "gx", 0, 0, tiled=True)
    vectors, sums = call(
        solve_kernel,
        (shape(8, rows, cols), shape(devices, LANES)),
        scratch=(
            pltpu.VMEM((FIELDS, ring + TILE, wide), jnp.float32),
            pltpu.VMEM((ring, wide), jnp.float32),
            pltpu.VMEM((ring, wide), jnp.float32),
            pltpu.VMEM((6, ring + TILE, wide), jnp.float32),
            pltpu.VMEM((4, ring + TILE, wide), jnp.float32),
            pltpu.VMEM((4, ring + TILE, wide), jnp.float32),
            pltpu.VMEM((6, ring, wide), jnp.float32),
        ),
        name="solve",
    )(own, tail, columns)
    table = lax.all_to_all(sums, ("gy", "gx"), 0, 0, tiled=True)
    return call(
        finish_kernel,
        (shape(2, rows, cols), shape(2, rows, cols), shape(rows, cols)),
        name="finish",
    )(table, own, vectors)


def solution(mesh):
    flat, both = P("gy", "gx"), P(None, "gy", "gx")
    return jax.shard_map(
        shards,
        mesh=mesh,
        in_specs=(flat, flat, flat, flat, both, both, both),
        out_specs=(both, both, flat),
        check_vma=False,
    )
```

time: 222 us -> 33.2 us (0.15)
  blocking collectives: 126 us -> 22.6 us
  starting transfers between devices: 48.5 us -> 4.32 us
  waiting for transfers between devices: 23.8 us -> 0.61 us
  between operations: 12.7 us -> 0.67 us
  other arithmetic: 8.04 us -> 0 us
  Pallas kernels: 0 us -> 4.78 us
    psum x3 -> x0, blocking collectives: 126 us -> none  [the longest x2 84.7 us: inner_sums(): fwd_total = lax.psum((fwd_local[0], fwd_local[1]), ('gy', 'gx'))]
    ppermute x20 -> x2, starting transfers between devices: 48.5 us -> 4.32 us  [the longest x1 3.03 us: swap(): lax.ppermute(to_next, axis, ahead)]
    ppermute x20 -> x2, waiting for transfers between devices: 23.8 us -> 0.61 us  [the longest x1 0.61 us: swap(): lax.ppermute(to_next, axis, ahead)]
    all_to_all x0 -> x2, blocking collectives: none -> 22.6 us  [the longest x1 12.8 us: shards(): table = lax.all_to_all(sums, ('gy', 'gx'), 0, 0, tiled=True)]
    pallas_call x0 -> x5, Pallas kernels: none -> 4.78 us  [the longest x1 1.99 us: shards(): call(solve_kernel, (shape(8, rows, cols), shape(devices, LANES)), scratch...]
    mul x12 -> x0, other arithmetic: 3.13 us -> none  [the longest x3 1.1 us: operate(): padded = padded_2(mask * field, (('gy', 1), ('gx', 2)), 1)]
  transfers between devices with their start and end apart: 20 -> 2, of which waited for: 9 -> 1; matrix products, arithmetic and copies ran while one was open for 0% -> 0% of each run, Pallas kernels for 0% -> 1%
where the time goes in v1:
time: 33.2 us; the launch traced here: 33 us
  blocking collectives  22.6 us (68%)
  Pallas kernels  4.78 us (14%)
  starting transfers between devices  4.32 us (13%)
  between operations  0.67 us (2%)
  waiting for transfers between devices  0.61 us (2%)
    all_to_all x1, blocking collectives, shards(): table = lax.all_to_all(sums, ('gy', 'gx'), 0, 0, tiled=True)  12.8 us
    all_to_all x1, blocking collectives, shards(): columns = lax.all_to_all(sends, 'gx', 0, 0, tiled=True)  9.81 us
    ppermute x1, starting transfers between devices, swap(): lax.ppermute(to_next, axis, ahead)  3.03 us
    pallas_call x1, Pallas kernels, shards(): call(solve_kernel, (shape(8, rows, cols), shape(devices, LANES)), scratch...  1.99 us
    ppermute x1, starting transfers between devices, swap(): lax.ppermute(to_previous, axis, back)  1.29 us
    pallas_call x1, Pallas kernels, shards(): call(pack_rows_kernel, (shape(ABOVE * FIELDS, cols), shape(BELOW * FIELDS...  1.25 us
    pallas_call x1, Pallas kernels, shards(): call(finish_kernel, (shape(2, rows, cols), shape(2, rows, cols), shape(ro...  1.24 us
  transfers between devices with their start and end apart: 2, of which 1 were waited for; matrix products, arithmetic and copies ran while one was open for 0% of the time, Pallas kernels for 1%

profile of v1, /device:TPU:0, one launch (start us, length us, event | category | flops | bytes accessed | tf_op | source)
XLA Modules:
  0.0 33.0 jit_solution(3156851263593264972)
XLA Ops:
  0.6 1.2 %pack_rows.1 = (f32[16,256]{1,0:T(8,128)S(1)}, f32[24,256]{1,0:T(8,128)S(1)}, s32[64,256]{1,0:T(8,128)S(1)}, s32[64,256]{1,0:T(8,128)S(1)}, f32[64,256]{1,0:T(8,...) custom-call(s32[64,256]{1,0:T(8,128)} %refs_0_.1, ...), custom_call_target="tpu_custom_call" | custom-call | tf_op jit(solution)/shard_map/pack_rows/pallas_call | solution.py:352
  1.9 1.3 %collective-permute-start.1 = (f32[24,256]{1,0:T(8,128)S(1)}, f32[24,256]{1,0:T(8,128)S(1)}, u32[]{:S(2)}, u32[]{:S(2)}) collective-permute-start(f32[24,256]{1,0:T(8,128)S(1)} %get-tuple-element.28), channel_id=1, source_target_pairs={{4,0},{8,4},{12,8},{16,12},{20,16},{24,20},{28,24},{5,1},{9,5},{13... | collective-permute-start | bytes 73736 | tf_op jit(solution)/shard_map/ppermute | solution.py:343
  3.2 3.0 %collective-permute-start = (f32[16,256]{1,0:T(8,128)S(1)}, f32[16,256]{1,0:T(8,128)S(1)}, u32[]{:S(2)}, u32[]{:S(2)}) collective-permute-start(f32[16,256]{1,0:T(8,128)S(1)} %get-tuple-element.27), channel_id=1, source_target_pairs={{0,4},{4,8},{8,12},{12,16},{16,20},{20,24},{24,28},{1,5},{5,9},{9,... | collective-permute-start | bytes 49160 | tf_op jit(solution)/shard_map/ppermute | solution.py:343
  6.2 0.2 fields.1
  6.4 0.6 %collective-permute-done.above = f32[16,256]{1,0:T(8,128)S(1)} collective-permute-done((f32[16,256]{1,0:T(8,128)S(1)}, f32[16,256]{1,0:T(8,128)S(1)}, u32[]{:S(2)}, u32[]{:S(2)}) %collective-permute-start) | collective-permute-done | bytes 16416 | tf_op jit(solution)/shard_map/ppermute | solution.py:343
  7.0 0.0 collective-permute-done.1.below
  7.1 0.1 tail.1
  7.2 9.8 %all_to_all.22 = f32[4,16,128]{2,1,0:T(8,128)S(1)} all-to-all(f32[4,16,128]{2,1,0:T(8,128)S(1)} %bitcast.8), channel_id=1, replica_groups=mesh['gy'=8,'gx'=4] {'gx'}, dimensions={0} | all-to-all | bytes 65536 | tf_op jit(solution)/shard_map/all_to_all | solution.py:371
  17.0 2.0 %solve.1 = (f32[8,64,256]{2,1,0:T(8,128)S(1)}, f32[32,128]{1,0:T(8,128)S(1)}) custom-call(f32[8,64,256]{2,1,0:T(8,128)S(1)} %get-tuple-element.26.own, f32[8,8,256]{2,1,0:T(8,128)S(1)} %get-tuple-element.31.tail, f32[64,128]{1,0:T(8,128)S(1)} %bitcast.6), custom_call_target="tpu_custom_call" | custom-call | tf_op jit(solution)/shard_map/solve/pallas_call | solution.py:372
  19.0 12.8 %all_to_all.23 = f32[32,1,128]{2,1,0:T(1,128)S(1)} all-to-all(f32[32,1,128]{2,1,0:T(1,128)S(1)} %bitcast.9), channel_id=1, replica_groups=mesh['gy'=8,'gx'=4] {'gy','gx'}, dimensions={0} | all-to-all | bytes 32768 | tf_op jit(solution)/shard_map/all_to_all | solution.py:386
  31.7 1.2 %finish.1 = (f32[2,64,256]{2,1,0:T(8,128)}, f32[2,64,256]{2,1,0:T(8,128)}, f32[64,256]{1,0:T(8,128)}) custom-call(f32[32,128]{1,0:T(8,128)S(1)} %bitcast.7, f32[8,64,256]{2,1,0:T(8,128)S(1)} %get-tuple-element.26.own, f32[8,64,256]{2,1,0:T(8,128)S(1)} %get-tuple-element.34.vectors), custom_call_target="tpu_custom_call" | custom-call | tf_op jit(solution)/shard_map/finish/pallas_call | solution.py:387
Async XLA Ops:
  1.9 5.2 %collective-permute-start.1 = (f32[24,256]{1,0:T(8,128)S(1)}, f32[24,256]{1,0:T(8,128)S(1)}, u32[]{:S(2)}, u32[]{:S(2)}) collective-permute-start(f32[24,256]{1,0:T(8,128)S(1)} %get-tuple-element.28), channel_id=1, source_target_pairs={{4,0},{8,4},{12,8},{16,12},{20,16},{24,20},{28,24},{5,1},{9,5},{13... | collective-permute-start | bytes 73736 | tf_op jit(solution)/shard_map/ppermute | solution.py:343
  3.2 3.9 %collective-permute-start = (f32[16,256]{1,0:T(8,128)S(1)}, f32[16,256]{1,0:T(8,128)S(1)}, u32[]{:S(2)}, u32[]{:S(2)}) collective-permute-start(f32[16,256]{1,0:T(8,128)S(1)} %get-tuple-element.27), channel_id=1, source_target_pairs={{0,4},{4,8},{8,12},{12,16},{16,20},{20,24},{24,28},{1,5},{5,9},{9,... | collective-permute-start | bytes 49160 | tf_op jit(solution)/shard_map/ppermute | solution.py:343

commit v2 on v1

v2 whole, which is shorter than its diff:
```python
import jax
import jax.numpy as jnp
from jax import lax
from jax.experimental import pallas as pl
from jax.experimental.pallas import tpu as pltpu
from jax.sharding import PartitionSpec as P

LANES = 128
TILE = 8
BELOW = 3
ABOVE = 2
FROM_LEFT = (2, 2, 2, 1, 1, 1, 2, 2)
FROM_RIGHT = (3, 3, 3, 1, 2, 2, 1, 1)
SLOT = 16
FIELDS = 8
GROUPS = LANES // SLOT
EDGE_TOP = 2
EDGE_BOTTOM = 3
SUMS = 7
SOLVE = 2
VMEM_LIMIT = 32 * 1024 * 1024


def derive(ice, grounded, thick, fric, prev, obs, drv):
    mask = ice.astype(jnp.float32)
    start_u = mask * prev[0]
    start_v = mask * prev[1]
    coef = mask * (grounded.astype(jnp.float32) * fric) + (1.0 - mask)
    return (
        start_u,
        start_v,
        mask * thick,
        coef,
        mask * drv[0],
        mask * drv[1],
        mask * (start_u - obs[0]),
        mask * (start_v - obs[1]),
    )


def read(refs, at):
    return [r[at, :] if len(r.shape) == 2 else r[:, at, :] for r in refs]


def add_columns(blocks, tile, fields):
    group, at_row, lane = *divmod(tile, blocks["tiles"]), blocks["lane"]
    east_at = west_at = SLOT * group
    for f, (first, last) in enumerate(fields):
        mine = (lane >= east_at) & (lane < east_at + FROM_LEFT[f])
        east = pltpu.roll(last, (east_at + FROM_LEFT[f]) % LANES, 1)
        blocks["east"][at_row] = jnp.where(mine, east, blocks["east"][at_row])
        if f in (4, 5):
            first = jnp.where(lane == 1, first - fields[3][0] * fields[f - 4][0], first)
        mine = (lane >= west_at) & (lane < west_at + FROM_RIGHT[f])
        west = pltpu.roll(first, west_at % LANES, 1)
        blocks["west"][at_row] = jnp.where(mine, west, blocks["west"][at_row])
        east_at, west_at = east_at + FROM_LEFT[f], west_at + FROM_RIGHT[f]


def new_blocks(east, west):
    lane = lax.broadcasted_iota(jnp.int32, (TILE, LANES), 1)
    return {"tiles": len(east), "lane": lane, "east": east, "west": west}


def block_tiles(rows):
    return -(-(rows // TILE) // GROUPS)


def pack_kernel(*refs):
    raw, (own, sends), held, arrived = refs[:7], refs[7:9], refs[9:16], refs[16]
    copies = [pltpu.make_async_copy(src, dst, arrived.at[i]) for i, (src, dst) in enumerate(zip(raw, held))]
    for copy in copies:
        copy.start()
    for copy in copies:
        copy.wait()
    rows, cols = own.shape[1:]
    height = block_tiles(rows)
    none = jnp.zeros((TILE, LANES), jnp.float32)
    blocks = new_blocks([none] * height, [none] * height)
    for tile in range(rows // TILE):
        at = pl.ds(TILE * tile, TILE)
        fields = derive(*read(held, at))
        for f, field in enumerate(fields):
            own[f, at, :] = field
        add_columns(blocks, tile, [(x[:, :LANES], x[:, cols - LANES :]) for x in fields])
    gx, count = lax.axis_index("gx"), lax.axis_size("gx")
    for i in range(count):
        to_next, to_previous = gx + 1 == i, gx - 1 == i
        for j in range(height):
            block = jnp.where(to_next, blocks["east"][j], jnp.where(to_previous, blocks["west"][j], 0.0))
            sends[pl.ds(TILE * (height * i + j), TILE), :] = block


def side_columns(columns, rows):
    gx, last = lax.axis_index("gx"), lax.axis_size("gx") - 1
    height = block_tiles(rows)
    lane = lax.broadcasted_iota(jnp.int32, (TILE, LANES), 1)

    def blocks(device, there):
        first = jnp.clip(device, 0, last) * (TILE * height)
        at = [pl.ds(pl.multiple_of(first + TILE * i, TILE), TILE) for i in range(height)]
        return [jnp.where(there, columns[a, :], 0.0) for a in at]

    left, right = blocks(gx - 1, gx > 0), blocks(gx + 1, gx < last)

    def side(f, tile):
        group, i = divmod(tile, height)
        before, after = FROM_LEFT[f], FROM_RIGHT[f]
        at = SLOT * group + sum(FROM_LEFT[:f])
        lanes = jnp.where(lane >= LANES - before, pltpu.roll(left[i], (2 * LANES - before - at) % LANES, 1), 0.0)
        at = SLOT * group + sum(FROM_RIGHT[:f])
        return jnp.where(lane < after, pltpu.roll(right[i], (LANES - at) % LANES, 1), lanes)

    return side


def rows_kernel(own, columns, ends, across, beside):
    rows, cols = own.shape[1:]
    last = rows // TILE - 1
    side = side_columns(columns, rows)
    even = lax.rem(lax.axis_index("gy"), 2) == 0
    for f in range(FIELDS):
        for tile, at in ((last, 0), (0, TILE)):
            ends[f, at : at + TILE, :cols] = own[f, TILE * tile : TILE * (tile + 1), :]
            ends[f, at : at + TILE, cols:] = side(f, tile)
        bottom, top = ends[f, TILE - BELOW : TILE, :], ends[f, TILE : TILE + BELOW, :]
        across[BELOW * f : BELOW * (f + 1), :] = jnp.where(even, top, bottom)
        beside[BELOW * f : BELOW * (f + 1), :] = jnp.where(even, bottom, top)


def to_right(x):
    return pltpu.roll(x, x.shape[1] - 1, 1)


def to_left(x):
    return pltpu.roll(x, 1, 1)


def gradient(u0, u1, v0, v1):
    us, ud = u1 + u0, u1 - u0
    vs, vd = v1 + v0, v1 - v0
    ux = to_right(us) - us
    uy = to_right(ud) + ud
    vx = to_right(vs) - vs
    vy = to_right(vd) + vd
    return ux, uy, vx, vy


def stress_of(weight, ux, vy, shear):
    return weight * (4.0 * ux + 2.0 * vy), weight * (4.0 * vy + 2.0 * ux), weight * shear


def fold(x):
    return sum(x[:, at : at + LANES] for at in range(0, x.shape[1], LANES))


def total(x):
    return jnp.sum(jnp.sum(x, axis=0, keepdims=True), axis=1, keepdims=True)


def sweep(scratch, own_corners, own_rows, theta, put):
    fld, wgt, strs, res, img, grd = scratch
    tiles = len(own_corners)
    wide = fld.shape[2]
    cols = wide - LANES
    blank = jnp.zeros((1, wide), jnp.float32)
    for ref, count, at in ((fld, 3, TILE * tiles), (res, 4, TILE * tiles), (img, 4, TILE * tiles), (strs, 9, TILE - 1)):
        for f in range(count):
            ref[f, at : at + 1, :] = blank

    def pair(ref, f, t):
        return ref[f, pl.ds(TILE * t, TILE), :], ref[f, pl.ds(TILE * t + 1, TILE), :]

    def put_stress(which, t, parts):
        for i, part in enumerate(parts):
            strs[3 * which + i, pl.ds(TILE * t + TILE, TILE), :] = part

    def operator(which, t, u, v):
        ux0, vy0, sh0 = [strs[3 * which + i, pl.ds(TILE * t + TILE, TILE), :] for i in range(3)]
        ux1, vy1, sh1 = [strs[3 * which + i, pl.ds(TILE * t + TILE - 1, TILE), :] for i in range(3)]
        a, b = ux0 + ux1, sh1 - sh0
        div_u = (b - a) + to_left(a + b)
        a, b = sh0 + sh1, vy1 - vy0
        div_v = (b - a) + to_left(a + b)
        at = pl.ds(TILE * t, TILE)
        ice, coef = fld[2, at, :] > 0.0, fld[3, at, :]
        return jnp.where(ice, div_u, 0.0) + coef * u, jnp.where(ice, div_v, 0.0) + coef * v

    for t in range(tiles):
        at = pl.ds(TILE * t, TILE)
        ux, uy, vx, vy = gradient(*pair(fld, 0, t), *pair(fld, 1, t))
        h0, h1 = pair(fld, 2, t)
        hs = h0 + h1
        hs = hs + to_right(hs)
        shear = uy + vx
        strain = ux * ux + vy * vy + ux * vy + 0.25 * (shear * shear)
        weight = (hs * 0.03125) * jnp.exp(jnp.log(0.25 * strain + 0.01) * (-1.0 / 3.0))
        wgt[at, :] = weight
        put_stress(0, t, stress_of(weight, ux, vy, shear))

    for t in range(tiles):
        at = pl.ds(TILE * t, TILE)
        image = operator(0, t, fld[0, at, :], fld[1, at, :])
        for i in range(2):
            res[i, at, :] = fld[4 + i, at, :] - image[i]
            res[2 + i, at, :] = fld[6 + i, at, :]

    for t in range(tiles):
        at = pl.ds(TILE * t, TILE)
        weight = wgt[at, :]
        for s in range(2):
            ux, uy, vx, vy = gradient(*pair(res, 2 * s, t), *pair(res, 2 * s + 1, t))
            shear = uy + vx
            grd[3 * s, at, :], grd[3 * s + 1, at, :], grd[3 * s + 2, at, :] = ux, vy, shear
            put_stress(1 + s, t, stress_of(weight, ux, vy, shear))
    dots = [jnp.zeros((TILE, cols), jnp.float32) for _ in range(4)]
    for t in range(tiles):
        at = pl.ds(TILE * t, TILE)
        for s in range(2):
            r = [res[2 * s + i, at, :] for i in range(2)]
            q = operator(1 + s, t, *r)
            for i in range(2):
                img[2 * s + i, at, :] = q[i]
                r_own, q_own = r[i][:, :cols], q[i][:, :cols]
                put(t, 4 * s + i, r_own)
                put(t, 4 * s + 2 + i, q_own)
                if own_rows[t] is not None:
                    r_own = jnp.where(own_rows[t], r_own, 0.0)
                dots[2 * s] = dots[2 * s] + r_own * r_own
                dots[2 * s + 1] = dots[2 * s + 1] + r_own * q_own
    dots = [fold(x) for x in dots]
    if theta is None:
        theta = []
        for s in range(2):
            norm, prod = total(dots[2 * s]), total(dots[2 * s + 1])
            some = norm > 0.0
            theta.append(jnp.where(some, prod / jnp.where(some, norm, 1.0), 0.0))

    size = [[jnp.zeros((TILE, cols), jnp.float32) for _ in range(2)] for _ in range(2)]
    energy = [[jnp.zeros((TILE, wide), jnp.float32) for _ in range(3)] for _ in range(2)]
    drag = [[jnp.zeros((TILE, cols), jnp.float32) for _ in range(3)] for _ in range(2)]
    for t in range(tiles):
        at = pl.ds(TILE * t, TILE)
        for s in range(2):
            weight = jnp.where(own_corners[t][s], wgt[at, :], 0.0)
            ux, uy, vx, vy = gradient(*pair(img, 2 * s, t), *pair(img, 2 * s + 1, t))
            rx, ry, rs = [grd[3 * s + i, at, :] for i in range(3)]
            wx, wy, ws = ux - theta[s] * rx, vy - theta[s] * ry, (uy + vx) - theta[s] * rs
            sx, sy, ss = stress_of(weight, wx, wy, ws)
            energy[s][0] = energy[s][0] + (sx * wx + sy * wy + ss * ws)
            energy[s][1] = energy[s][1] + (sx * rx + sy * ry + ss * rs)
            sx, sy, ss = stress_of(weight, rx, ry, rs)
            energy[s][2] = energy[s][2] + (sx * rx + sy * ry + ss * rs)
            coef = fld[3, at, :cols]
            for i in range(2):
                r = res[2 * s + i, at, :cols]
                w = img[2 * s + i, at, :cols] - theta[s] * r
                if own_rows[t] is not None:
                    r, w = jnp.where(own_rows[t], r, 0.0), jnp.where(own_rows[t], w, 0.0)
                ww, wr = w * w, w * r
                size[s][0], size[s][1] = size[s][0] + ww, size[s][1] + wr
                drag[s][0] = drag[s][0] + coef * ww
                drag[s][1] = drag[s][1] + coef * wr
                drag[s][2] = drag[s][2] + coef * (r * r)
    sums = []
    for s in range(2):
        sums += [dots[2 * s], dots[2 * s + 1], fold(size[s][0]), fold(size[s][1])]
        sums += [fold(energy[s][i]) + fold(drag[s][i]) for i in range(3)]
    return sums, theta


def own_columns(wide):
    col = lax.broadcasted_iota(jnp.int32, (TILE, wide), 1)
    cols = wide - LANES
    gx, end = lax.axis_index("gx"), lax.axis_size("gx") - 1
    inside, left, right = col < cols - 1, col == wide - 1, col == cols - 1
    return inside | right | (left & (gx == 0)), inside | left | (right & (gx == end))


def row_masks(wide, first, last):
    row = lax.broadcasted_iota(jnp.int32, (TILE, wide), 0)
    rows = (row >= first) & (row <= last)
    return rows, rows[:, : wide - LANES]


def inner_kernel(own, columns, vectors, partial, theta, *scratch):
    fld = scratch[0]
    rows, cols = own.shape[1:]
    wide, tiles = cols + LANES, rows // TILE
    side = side_columns(columns, rows)
    for f in range(FIELDS):
        for t in range(tiles):
            at = pl.ds(TILE * t, TILE)
            fld[f, at, :cols] = own[f, at, :]
            fld[f, at, cols:] = side(f, t)
    corners, cells = [own_columns(wide)] * tiles, [None] * tiles
    for t, first, last in ((0, EDGE_TOP, TILE - 1), (tiles - 1, 0, TILE - 1 - EDGE_BOTTOM)):
        all_lanes, cells[t] = row_masks(wide, first, last)
        corners[t] = [x & all_lanes for x in corners[t]]

    def put(t, which, value):
        vectors[which, TILE * t : TILE * (t + 1), :] = value

    sums, thetas = sweep(scratch, corners, cells, None, put)
    for i, x in enumerate(sums):
        partial[i] = x
    for i, x in enumerate(thetas):
        theta[i] = jnp.broadcast_to(x, (TILE, LANES))


def outer_kernel(ends, across, beside, partial, theta, edges, sums, *scratch):
    fld = scratch[0]
    wide = ends.shape[2]
    even = lax.rem(lax.axis_index("gy"), 2) == 0
    kept = TILE - BELOW
    for f in range(FIELDS):
        a, b = across[BELOW * f : BELOW * (f + 1), :], beside[BELOW * f : BELOW * (f + 1), :]
        below, above = jnp.where(even, b, a), jnp.where(even, a, b)
        fld[f, 0:kept, :] = ends[f, TILE - kept : TILE, :]
        fld[f, kept:TILE, :] = below
        fld[f, TILE : TILE + ABOVE, :] = above[BELOW - ABOVE :]
        fld[f, TILE + ABOVE : 2 * TILE, :] = ends[f, TILE : 2 * TILE - ABOVE, :]
    mine = own_columns(wide)
    low, low_cells = row_masks(wide, kept - EDGE_BOTTOM, kept - 1)
    high, high_cells = row_masks(wide, ABOVE, ABOVE + EDGE_TOP - 1)
    row = lax.broadcasted_iota(jnp.int32, (TILE, wide), 0)
    high = high | ((row == ABOVE - 1) & (lax.axis_index("gy") == 0))

    def put(t, which, value):
        if t == 0:
            edges[which, 2 * TILE - EDGE_BOTTOM : 2 * TILE, :] = value[kept - EDGE_BOTTOM : kept]
        else:
            edges[which, 0:EDGE_TOP, :] = value[ABOVE : ABOVE + EDGE_TOP]

    mixed = [theta[i][0:1, 0:1] for i in range(2)]
    made, _ = sweep(scratch, [[x & low for x in mine], [x & high for x in mine]], [low_cells, high_cells], mixed, put)
    row = lax.broadcasted_iota(jnp.int32, (2 * TILE, LANES), 0)
    stack = jnp.zeros((2 * TILE, LANES), jnp.float32)
    for i, value in enumerate(made):
        stack = jnp.where(row == i, jnp.sum(value + partial[i], axis=0, keepdims=True), stack)
    stack = jnp.sum(stack, axis=1, keepdims=True)
    for i in range(2):
        stack = jnp.where(row[:, 0:1] == len(made) + i, mixed[i], stack)
    lane = lax.broadcasted_iota(jnp.int32, (2 * TILE, LANES), 1)
    solve, which = row // SUMS, lax.rem(row, SUMS)
    place = jnp.where(row < 2 * SUMS, SOLVE * which + solve, SOLVE * SUMS + row - 2 * SUMS)
    line = jnp.sum(jnp.where(lane == place, stack, 0.0), axis=0, keepdims=True)
    sums[...] = jnp.broadcast_to(line, sums.shape)


def steps_of(table):
    def column(x, i):
        return pltpu.roll(x, (LANES - SOLVE * i) % LANES, 1)

    def over(x):
        return jnp.sum(x, axis=0, keepdims=True)

    used = lax.broadcasted_iota(jnp.int32, (1, LANES), 1) < 2
    norm_d, _, size, cross, ww, rw, rr, theta_d = [column(table, i) for i in range(SUMS + 1)]
    sums = over(table)
    norm, prod = [jnp.where(used, column(sums, i), 1.0) for i in range(2)]
    alpha = norm / prod
    shift = theta_d - prod / norm
    square = alpha * alpha
    norm_1 = square * over(size + shift * (2.0 * cross + shift * norm_d))
    prod_1 = square * over(ww + shift * (2.0 * rw + shift * rr))
    ratio = norm_1 / norm
    some = used & (norm_1 > 0.0)
    bottom = jnp.where(some, prod_1 - ratio * norm_1 / alpha, 1.0)
    return alpha, ratio, jnp.where(some, norm_1, 0.0) / bottom


def finish_kernel(table, own, vectors, edges, velocity, adjoint, grad):
    found = steps_of(table[...])
    steps = [[x[:, s : s + 1] for x in found] for s in range(2)]
    rows, cols = own.shape[1:]
    last = rows // TILE - 1
    row = lax.broadcasted_iota(jnp.int32, (TILE, cols), 0)
    for t in range(last + 1):
        at = pl.ds(TILE * t, TILE)

        def vector(which):
            x = vectors[which, at, :]
            if t == 0:
                x = jnp.where(row < EDGE_TOP, edges[which, 0:TILE, :], x)
            if t == last:
                x = jnp.where(row >= TILE - EDGE_BOTTOM, edges[which, TILE : 2 * TILE, :], x)
            return x

        made = []
        for s in range(2):
            alpha, ratio, alpha_1 = steps[s]
            for i in range(2):
                r, q = vector(4 * s + i), vector(4 * s + 2 + i)
                step = alpha * r + alpha_1 * ((r - alpha * q) + ratio * r)
                made.append(own[i, at, :] + step if s == 0 else step)
        friction = jnp.where(own[2, at, :] > 0.0, own[3, at, :], 0.0)
        velocity[0, at, :], velocity[1, at, :] = made[0], made[1]
        adjoint[0, at, :], adjoint[1, at, :] = made[2], made[3]
        grad[at, :] = -friction * (made[0] * made[2] + made[1] * made[3])


def shape(*dims):
    return jax.ShapeDtypeStruct(dims, jnp.float32)


def call(kernel, outs, scratch=(), **kwargs):
    return pl.pallas_call(
        kernel,
        out_shape=outs,
        scratch_shapes=scratch,
        compiler_params=pltpu.CompilerParams(vmem_limit_bytes=VMEM_LIMIT),
        **kwargs,
    )


def sweep_scratch(tiles, wide):
    rows = TILE * tiles
    deep = [pltpu.VMEM((n, rows + TILE, wide), jnp.float32) for n in (FIELDS, 9, 4, 4)]
    return [deep[0], pltpu.VMEM((rows, wide), jnp.float32), *deep[1:], pltpu.VMEM((6, rows, wide), jnp.float32)]


def swap(x, axis, first):
    pairs = [(i, i + 1) for i in range(first, lax.axis_size(axis) - 1, 2)]
    return lax.ppermute(x, axis, pairs + [(j, i) for i, j in pairs])


def shards(ice_mask, grounded, thickness, friction, previous_velocity, observed, driving):
    raw = (ice_mask, grounded, thickness, friction, previous_velocity, observed, driving)
    rows, cols = ice_mask.shape
    wide, tiles = cols + LANES, rows // TILE
    devices = lax.axis_size(("gy", "gx"))
    own, sends = call(
        pack_kernel,
        (shape(FIELDS, rows, cols), shape(lax.axis_size("gx") * TILE * block_tiles(rows), LANES)),
        scratch=[pltpu.VMEM(x.shape, x.dtype) for x in raw] + [pltpu.SemaphoreType.DMA((len(raw),))],
        in_specs=[pl.BlockSpec(memory_space=pltpu.HBM)] * len(raw),
        name="pack",
    )(*[pltpu.with_memory_space_constraint(x, pltpu.HBM) for x in raw])
    columns = lax.all_to_all(sends, "gx", 0, 0, tiled=True)
    ends, across, beside = call(
        rows_kernel,
        (shape(FIELDS, 2 * TILE, wide), shape(BELOW * FIELDS, wide), shape(BELOW * FIELDS, wide)),
        name="rows",
    )(own, columns)
    across = swap(across, "gy", 1)
    beside = swap(beside, "gy", 0)
    vectors, partial, theta = call(
        inner_kernel,
        (
            shape(8, rows, cols),
            shape(2 * SUMS, TILE, LANES),
            shape(2, TILE, LANES),
        ),
        scratch=sweep_scratch(tiles, wide),
        cost_estimate=pl.CostEstimate(flops=500 * rows * wide, bytes_accessed=64 * rows * wide, transcendentals=0),
        name="inner",
    )(own, columns)
    edges, sums = call(
        outer_kernel,
        (shape(8, 2 * TILE, cols), shape(devices, LANES)),
        scratch=sweep_scratch(2, wide),
        name="outer",
    )(ends, across, beside, partial, theta)
    table = lax.all_to_all(sums, ("gy", "gx"), 0, 0, tiled=True)
    return call(
        finish_kernel,
        (shape(2, rows, cols), shape(2, rows, cols), shape(rows, cols)),
        name="finish",
    )(table, own, vectors, edges)


def solution(mesh):
    flat, both = P("gy", "gx"), P(None, "gy", "gx")
    return jax.shard_map(
        shards,
        mesh=mesh,
        in_specs=(flat, flat, flat, flat, both, both, both),
        out_specs=(both, both, flat),
        check_vma=False,
    )
```

time: 33.2 us -> 30.1 us (0.907)
  blocking collectives: 22.6 us -> 20.5 us
  starting transfers between devices: 4.32 us -> 3.67 us
  waiting for transfers between devices: 0.61 us -> 0.01 us
    all_to_all x1, blocking collectives: 12.8 us -> 10.8 us  [shards(): table = lax.all_to_all(sums, ('gy', 'gx'), 0, 0, tiled=True)]
    ppermute x2, starting transfers between devices: 4.32 us -> 3.67 us  [swap(): return lax.ppermute(x, axis, pairs + [(j, i) for i, j in pairs])]
    ppermute x2, waiting for transfers between devices: 0.61 us -> 0.01 us  [swap(): return lax.ppermute(x, axis, pairs + [(j, i) for i, j in pairs])]
    pallas_call x4, Pallas kernels: 3.54 us -> 4.05 us  [the longest x1 1.72 us: shards(): call(inner_kernel, (shape(8, rows, cols), shape(2 * SUMS, TILE, LANES), s...]
  transfers between devices with their start and end apart: 2 -> 2, of which waited for: 1 -> 0; matrix products, arithmetic and copies ran while one was open for 0% -> 0% of each run, Pallas kernels for 1% -> 6%
where the time goes in v2:
time: 30.1 us; the launch traced here: 29.8 us
  blocking collectives  20.5 us (68%)
  Pallas kernels  4.97 us (17%)
  starting transfers between devices  3.67 us (12%)
  between operations  0.68 us (2%)
    all_to_all x1, blocking collectives, shards(): table = lax.all_to_all(sums, ('gy', 'gx'), 0, 0, tiled=True)  10.8 us
    all_to_all x1, blocking collectives, shards(): columns = lax.all_to_all(sends, 'gx', 0, 0, tiled=True)  9.68 us
    ppermute x2, starting transfers between devices, swap(): return lax.ppermute(x, axis, pairs + [(j, i) for i, j in pairs])  3.67 us
    pallas_call x1, Pallas kernels, shards(): call(inner_kernel, (shape(8, rows, cols), shape(2 * SUMS, TILE, LANES), s...  1.72 us
    pallas_call x1, Pallas kernels, shards(): call(pack_kernel, (shape(FIELDS, rows, cols), shape(lax.axis_size('gx') *...  1.44 us
    pallas_call x1, Pallas kernels, shards(): call(finish_kernel, (shape(2, rows, cols), shape(2, rows, cols), shape(ro...  0.92 us
    pallas_call x1, Pallas kernels, shards(): call(outer_kernel, (shape(8, 2 * TILE, cols), shape(devices, LANES)), scr...  0.78 us
  transfers between devices with their start and end apart: 2, of which 0 were waited for; matrix products, arithmetic and copies ran while one was open for 0% of the time, Pallas kernels for 6%

profile of v2, /device:TPU:0, one launch (start us, length us, event | category | flops | bytes accessed | tf_op | source)
XLA Modules:
  0.0 29.8 jit_solution(16628177927024185522)
XLA Ops:
  0.6 1.4 %pack.1 = (f32[8,64,256]{2,1,0:T(8,128)S(1)}, f32[32,128]{1,0:T(8,128)S(1)}) custom-call(s32[64,256]{1,0:T(8,128)} %refs_0_.1, s32[64,256]{1,0:T(8,128)} %refs_1_.1, f32[64,256]{1,0:T(8,128)} %refs_2_.1, f32[64,256]{1,0:T(8,128)} %refs_3_.1, f32[2,64,256]{2,1,0:T(8,128)} %refs_4_.1, f32[2,64,256]{2,1,0:T(8,128)} %refs_5_.1, f32[2,64,256]{2,1,0:T(8,128)} %refs_6_.1), custom_call_target="tpu_custom_call" | custom-call | tf_op jit(solution)/shard_map/pack/pallas_call | solution.py:433
  2.1 9.7 %all_to_all.22 = f32[4,8,128]{2,1,0:T(8,128)S(1)} all-to-all(f32[4,8,128]{2,1,0:T(8,128)S(1)} %bitcast.10), channel_id=1, replica_groups=mesh['gy'=8,'gx'=4] {'gx'}, dimensions={0} | all-to-all | bytes 32768 | tf_op jit(solution)/shard_map/all_to_all | solution.py:440
  11.8 0.1 rows.1
  11.9 0.7 %collective-permute-start = (f32[24,384]{1,0:T(8,128)S(1)}, f32[24,384]{1,0:T(8,128)S(1)}, u32[]{:S(2)}, u32[]{:S(2)}) collective-permute-start(f32[24,384]{1,0:T(8,128)S(1)} %get-tuple-element.16), channel_id=1, source_target_pairs={{4,8},{12,16},{20,24},{8,4},{16,12},{24,20},{5,9},{13,17},{21,25},... | collective-permute-start | bytes 110600 | tf_op jit(solution)/shard_map/ppermute | solution.py:425
  12.6 3.0 %collective-permute-start.1 = (f32[24,384]{1,0:T(8,128)S(1)}, f32[24,384]{1,0:T(8,128)S(1)}, u32[]{:S(2)}, u32[]{:S(2)}) collective-permute-start(f32[24,384]{1,0:T(8,128)S(1)} %get-tuple-element.17), channel_id=1, source_target_pairs={{0,4},{8,12},{16,20},{24,28},{4,0},{12,8},{20,16},{28,24},{1,5},{9... | collective-permute-start | bytes 110600 | tf_op jit(solution)/shard_map/ppermute | solution.py:425
  15.6 1.7 %inner.1 = (f32[8,64,256]{2,1,0:T(8,128)S(1)}, f32[14,8,128]{2,1,0:T(8,128)S(1)}, f32[2,8,128]{2,1,0:T(8,128)S(1)}) custom-call(f32[8,64,256]{2,1,0:T(8,128)S(1)} %get-tuple-element.13.own, f32[32,128]{1,0:T(8,128)S(1)} %bitcast.7), custom_call_target="tpu_custom_call" | custom-call | flops 12288000 | bytes 1572864 | tf_op jit(solution)/shard_map/inner/pallas_call | solution.py:448
  17.3 0.0 collective-permute-done.across
  17.3 0.0 collective-permute-done.1.beside
  17.3 0.8 %outer.1 = (f32[8,16,256]{2,1,0:T(8,128)S(1)}, f32[32,128]{1,0:T(8,128)S(1)}) custom-call(f32[8,16,384]{2,1,0:T(8,128)S(1)} %get-tuple-element.15.ends, f32[24,384]{1,0:T(8,128)S(1)} %collective-permute-done.across, f32[24,384]{1,0:T(8,128)S(1)} %collective-permute-done.1.beside, f32[14,8,128]{2,1,0:T(8,128)S(1)} %get-tuple-element.18.partial, ...), custom_call_target="tpu_custom_call" | custom-call | tf_op jit(solution)/shard_map/outer/pallas_call | solution.py:459
  18.1 10.8 %all_to_all.23 = f32[32,1,128]{2,1,0:T(1,128)S(1)} all-to-all(f32[32,1,128]{2,1,0:T(1,128)S(1)} %bitcast.9), channel_id=1, replica_groups=mesh['gy'=8,'gx'=4] {'gy','gx'}, dimensions={0} | all-to-all | bytes 32768 | tf_op jit(solution)/shard_map/all_to_all | solution.py:465
  28.9 0.9 %finish.1 = (f32[2,64,256]{2,1,0:T(8,128)}, f32[2,64,256]{2,1,0:T(8,128)}, f32[64,256]{1,0:T(8,128)}) custom-call(f32[32,128]{1,0:T(8,128)S(1)} %bitcast.8, f32[8,64,256]{2,1,0:T(8,128)S(1)} %get-tuple-element.13.own, f32[8,64,256]{2,1,0:T(8,128)S(1)} %get-tuple-element.21.vectors, f32[8,16,256]{2,1,0:T(8,128)S(1)} %get-tuple-element.22.edges), custom_call_target="tpu_custom_call" | custom-call | tf_op jit(solution)/shard_map/finish/pallas_call | solution.py:466
Async XLA Ops:
  11.9 5.4 %collective-permute-start = (f32[24,384]{1,0:T(8,128)S(1)}, f32[24,384]{1,0:T(8,128)S(1)}, u32[]{:S(2)}, u32[]{:S(2)}) collective-permute-start(f32[24,384]{1,0:T(8,128)S(1)} %get-tuple-element.16), channel_id=1, source_target_pairs={{4,8},{12,16},{20,24},{8,4},{16,12},{24,20},{5,9},{13,17},{21,25},... | collective-permute-start | bytes 110600 | tf_op jit(solution)/shard_map/ppermute | solution.py:425
  12.6 4.7 %collective-permute-start.1 = (f32[24,384]{1,0:T(8,128)S(1)}, f32[24,384]{1,0:T(8,128)S(1)}, u32[]{:S(2)}, u32[]{:S(2)}) collective-permute-start(f32[24,384]{1,0:T(8,128)S(1)} %get-tuple-element.17), channel_id=1, source_target_pairs={{0,4},{8,12},{16,20},{24,28},{4,0},{12,8},{20,16},{28,24},{1,5},{9... | collective-permute-start | bytes 110600 | tf_op jit(solution)/shard_map/ppermute | solution.py:425
